TPU v7x, 512 devices: a whole 4x8x8 slice. The times are simulated.
512 devices in a mesh: node: 16 (over y, z_lo), cross: 32 (over z_hi, x, core).
Axes of the slice: x: 4, y: 8, z: 8 (z_hi: 4, z_lo: 2; z = z_hi * 2 + z_lo), core: 2. Of those that a mesh axis runs over, the one named last changes fastest.
Arguments:
- tokens: bfloat16 [4096, 5120], P('node', 'cross'), may hold values from -6 to 6
- weight_codes: int32 [5120, 20480], P('node', 'cross'), may hold values from -127 to 127
- weight_scales: float32 [5120, 160], P('node', 'cross'), may hold values from 5e-05 to 0.0004
- cotangent: bfloat16 [4096, 20480], P('node', 'cross'), may hold values from -6 to 6
- grad_exponents: int32 [5120, 160], P('node', 'cross'), may hold values from 6 to 9
Outputs:
- projected: bfloat16 [4096, 20480], P('node', 'cross')
- token_grad: bfloat16 [4096, 5120], P('node', 'cross')
- weight_grad: float32 [5120, 20480], P('node', 'cross')
All inputs are finite; a program needn't handle non-finite values.
Results may differ from a plain program's by a relative error of at most 0.019.
Values may be sent and summed in bfloat16 or wider, within the bound.
A program may use at most 64 MiB of HBM per device.

v0:
```python
import jax
import jax.numpy as jnp
from jax import lax
from jax.sharding import PartitionSpec as P

QBLOCK = 128


def on_device(tokens, weight_codes, weight_scales, cotangent, grad_exponents):
    weight_own = (
        weight_codes.astype(jnp.float32) * jnp.repeat(weight_scales, QBLOCK, axis=1)
    ).astype(jnp.bfloat16)
    features = lax.all_gather(tokens, "cross", axis=1, tiled=True)
    row_count = weight_codes.shape[0]
    col_count = weight_codes.shape[1]
    node_count = lax.axis_size("node")
    piece = lax.all_gather(weight_own, "node", axis=0, tiled=True)
    forward = jnp.dot(features, piece, preferred_element_type=jnp.float32)
    image = lax.dot_general(
        cotangent, piece, (((1,), (1,)), ((), ())), preferred_element_type=jnp.float32
    )
    backward = image
    forward, backward = (forward, backward)
    projected = forward.astype(jnp.bfloat16)
    token_grad = lax.psum_scatter(
        backward.astype(jnp.bfloat16), "cross", scatter_dimension=1, tiled=True
    )
    block_count = col_count // QBLOCK

    def grad_block(carry, index):
        start = index * QBLOCK
        cot_columns = lax.dynamic_slice_in_dim(cotangent, start, QBLOCK, 1)
        partial_term = lax.dot_general(
            features, cot_columns, (((0,), (0,)), ((), ())), preferred_element_type=jnp.float32
        ).astype(jnp.bfloat16)
        partial_term = partial_term.reshape(node_count, row_count, QBLOCK)
        received = lax.all_to_all(partial_term, "node", split_axis=0, concat_axis=0, tiled=True)
        return (carry, jnp.sum(received.astype(jnp.float32), axis=0))

    _, pieces = lax.scan(
        grad_block, jnp.zeros((), jnp.float32), jnp.arange(block_count, dtype=jnp.int32)
    )
    grad_sum = pieces.transpose(1, 0, 2).reshape(row_count, col_count)
    factor = jnp.exp2(-jnp.repeat(grad_exponents, QBLOCK, axis=1).astype(jnp.float32))
    weight_grad = grad_sum * factor
    return (projected, token_grad, weight_grad)


def solution(mesh):
    placed = (
        P("node", "cross"),
        P("node", "cross"),
        P("node", "cross"),
        P("node", "cross"),
        P("node", "cross"),
    )
    return jax.shard_map(
        on_device,
        mesh=mesh,
        in_specs=placed,
        out_specs=(P("node", "cross"), P("node", "cross"), P("node", "cross")),
        check_vma=False,
    )
```

profile of v0, /device:TPU:1, one launch (start us, length us, event | category | flops | bytes accessed | tf_op | source)
XLA Modules:
  0.0 465.6 jit_solution(17406180319164219370)
XLA Ops:
  7.2 0.7 all-gather.5.cloned.1.call-update
  8.0 0.8 broadcast_in_dim.13
  8.7 0.3 copy.26
  9.1 0.8 multiply_convert_fusion
  10.0 68.9 %all-gather.5.cloned.1.call-done = bf16[256,5120]{0,1:T(8,128)(2,1)} async-done(((bf16[256,160]{0,1:T(8,128)(2,1)}), bf16[256,5120]{0,1:T(8,128)(2,1)}) %all-gather.5.cloned.1.call-update) | async-done | bytes 2621456 | tf_op jit(solution)/shard_map/all_gather | solution.py:13
  79.0 4.5 copy.27
  83.4 142.8 %all-gather.3.cloned.1.call-done = bf16[5120,640]{1,0:T(8,128)(2,1)} async-done(((bf16[320,640]{1,0:T(8,128)(2,1)}), bf16[5120,640]{1,0:T(8,128)(2,1)}) %all-gather.3.cloned.1.call-update) | async-done | bytes 6553616 | tf_op jit(solution)/shard_map/all_gather | solution.py:17
  226.3 6.6 %fusion.3 = bf16[256,5120]{0,1:T(8,128)(2,1)} fusion(bf16[5120,640]{1,0:T(8,128)(2,1)} %all-gather.3.cloned.1.call-done, bf16[256,640]{1,0:T(8,128)(2,1)S(1)} %copy-done.2), kind=kOutput, calls=%fused_computation.7 | convolution fusion | flops 1679032320 | bytes 9502720 | tf_op jit(solution)/shard_map/dot_general | solution.py:19
  232.9 215.2 %while.10 = (s32[]{:T(128)}, f32[5,320,128]{2,1,0:T(8,128)}, s32[5]{0:T(128)S(1)}, bf16[256,640]{1,0:T(8,128)(2,1)S(1)}, bf16[256,5120]{1,0:T(8,128)(2,1)}, /*index=5*/s32[]{:T(128)}, s32[1]{0:T(128)}, s32[]{:T(128)}, s32[]{:T(128)}) while((s32[]{:T(128)}, f32[5,320,128]{2,1,0:T(8,128)}, s32[5]{0:T(128)S(1)}, bf16[256,640]{1,0:T(8,128)(2,1)S(1)}, ...), condition=%wide.region_3.4_spmd, body=%wide.region_1.3_spmd.sunk | while | flops 337469440 | bytes 12353735 | solution.py:40
  232.9 0.6 dynamic_slice.12
  234.2 2.3 fusion.15
  236.5 1.4 copy.32
  237.9 6.8 %all-to-all-start = ((bf16[16,320,128]{2,1,0:T(8,128)(2,1)}), bf16[16,320,128]{2,1,0:T(8,128)(2,1)S(1)}, u32[]{:S(2)}, u32[]{:S(2)}) async-start(bf16[16,320,128]{2,1,0:T(8,128)(2,1)} %bitcast.28), calls=%async_computation | async-start | bytes 2621440 | tf_op jit(solution)/shard_map/while/body/eval_jaxpr/all_to_all | solution.py:37
  244.7 30.0 %all-to-all-done = bf16[16,320,128]{2,1,0:T(8,128)(2,1)S(1)} async-done(((bf16[16,320,128]{2,1,0:T(8,128)(2,1)}), bf16[16,320,128]{2,1,0:T(8,128)(2,1)S(1)}, u32[]{:S(2)}, u32[]{:S(2)}) %all-to-all-start) | async-done | bytes 1310752 | tf_op jit(solution)/shard_map/while/body/eval_jaxpr/all_to_all | solution.py:37
  274.6 0.2 convert_reduce_fusion.2
  274.8 0.7 bitcast_dynamic-update-slice_fusion.2
  275.5 0.6 dynamic_slice.12
  276.7 2.3 fusion.15
  279.0 1.4 copy.32
  280.5 7.3 %all-to-all-start = ((bf16[16,320,128]{2,1,0:T(8,128)(2,1)}), bf16[16,320,128]{2,1,0:T(8,128)(2,1)S(1)}, u32[]{:S(2)}, u32[]{:S(2)}) async-start(bf16[16,320,128]{2,1,0:T(8,128)(2,1)} %bitcast.28), calls=%async_computation | async-start | bytes 2621440 | tf_op jit(solution)/shard_map/while/body/eval_jaxpr/all_to_all | solution.py:37
  287.8 29.9 %all-to-all-done = bf16[16,320,128]{2,1,0:T(8,128)(2,1)S(1)} async-done(((bf16[16,320,128]{2,1,0:T(8,128)(2,1)}), bf16[16,320,128]{2,1,0:T(8,128)(2,1)S(1)}, u32[]{:S(2)}, u32[]{:S(2)}) %all-to-all-start) | async-done | bytes 1310752 | tf_op jit(solution)/shard_map/while/body/eval_jaxpr/all_to_all | solution.py:37
  317.6 0.2 convert_reduce_fusion.2
  317.8 0.7 bitcast_dynamic-update-slice_fusion.2
  318.5 0.6 dynamic_slice.12
  319.7 2.3 fusion.15
  322.0 1.4 copy.32
  323.5 7.7 %all-to-all-start = ((bf16[16,320,128]{2,1,0:T(8,128)(2,1)}), bf16[16,320,128]{2,1,0:T(8,128)(2,1)S(1)}, u32[]{:S(2)}, u32[]{:S(2)}) async-start(bf16[16,320,128]{2,1,0:T(8,128)(2,1)} %bitcast.28), calls=%async_computation | async-start | bytes 2621440 | tf_op jit(solution)/shard_map/while/body/eval_jaxpr/all_to_all | solution.py:37
  331.2 29.8 %all-to-all-done = bf16[16,320,128]{2,1,0:T(8,128)(2,1)S(1)} async-done(((bf16[16,320,128]{2,1,0:T(8,128)(2,1)}), bf16[16,320,128]{2,1,0:T(8,128)(2,1)S(1)}, u32[]{:S(2)}, u32[]{:S(2)}) %all-to-all-start) | async-done | bytes 1310752 | tf_op jit(solution)/shard_map/while/body/eval_jaxpr/all_to_all | solution.py:37
  361.0 0.2 convert_reduce_fusion.2
  361.2 0.7 bitcast_dynamic-update-slice_fusion.2
  361.9 0.6 dynamic_slice.12
  363.1 2.3 fusion.15
  365.4 1.4 copy.32
  366.9 7.4 %all-to-all-start = ((bf16[16,320,128]{2,1,0:T(8,128)(2,1)}), bf16[16,320,128]{2,1,0:T(8,128)(2,1)S(1)}, u32[]{:S(2)}, u32[]{:S(2)}) async-start(bf16[16,320,128]{2,1,0:T(8,128)(2,1)} %bitcast.28), calls=%async_computation | async-start | bytes 2621440 | tf_op jit(solution)/shard_map/while/body/eval_jaxpr/all_to_all | solution.py:37
  374.3 29.9 %all-to-all-done = bf16[16,320,128]{2,1,0:T(8,128)(2,1)S(1)} async-done(((bf16[16,320,128]{2,1,0:T(8,128)(2,1)}), bf16[16,320,128]{2,1,0:T(8,128)(2,1)S(1)}, u32[]{:S(2)}, u32[]{:S(2)}) %all-to-all-start) | async-done | bytes 1310752 | tf_op jit(solution)/shard_map/while/body/eval_jaxpr/all_to_all | solution.py:37
  404.2 0.2 convert_reduce_fusion.2
  404.4 0.7 bitcast_dynamic-update-slice_fusion.2
  405.0 0.6 dynamic_slice.12
  406.3 2.3 fusion.15
  408.6 1.4 copy.32
  410.0 7.4 %all-to-all-start = ((bf16[16,320,128]{2,1,0:T(8,128)(2,1)}), bf16[16,320,128]{2,1,0:T(8,128)(2,1)S(1)}, u32[]{:S(2)}, u32[]{:S(2)}) async-start(bf16[16,320,128]{2,1,0:T(8,128)(2,1)} %bitcast.28), calls=%async_computation | async-start | bytes 2621440 | tf_op jit(solution)/shard_map/while/body/eval_jaxpr/all_to_all | solution.py:37
  417.4 29.8 %all-to-all-done = bf16[16,320,128]{2,1,0:T(8,128)(2,1)S(1)} async-done(((bf16[16,320,128]{2,1,0:T(8,128)(2,1)}), bf16[16,320,128]{2,1,0:T(8,128)(2,1)S(1)}, u32[]{:S(2)}, u32[]{:S(2)}) %all-to-all-start) | async-done | bytes 1310752 | tf_op jit(solution)/shard_map/while/body/eval_jaxpr/all_to_all | solution.py:37
  447.5 0.7 bitcast_dynamic-update-slice_fusion.2
  448.1 1.6 bitcast_multiply_fusion
  449.7 1.3 copy.28
  451.0 2.4 copy.30
  453.4 4.8 %fusion.4 = bf16[256,640]{0,1:T(8,128)(2,1)S(1)} fusion(bf16[5120,640]{1,0:T(8,128)(2,1)} %all-gather.3.cloned.1.call-done, bf16[256,5120]{0,1:T(8,128)(2,1)S(1)} %copy-done), kind=kOutput, calls=%fused_computation.9 | convolution fusion | flops 1677885440 | bytes 9502720 | tf_op jit(solution)/shard_map/dot_general | solution.py:18
  458.2 0.9 copy.29
  (18 shorter events, 0.4 us)
Async XLA Ops:
  7.2 1.9 copy-start.1
  7.2 71.8 %all-gather.5.cloned.1.call-start = ((), (), s32[]{:S(2)}) async-start(), calls=%async_computation.3 | async-start | bytes 2703360 | tf_op jit(solution)/shard_map/all_gather | solution.py:13
  7.9 2.1 copy-start.3
  7.9 218.3 %all-gather.3.cloned.1.call-start = ((), (), s32[]{:S(2)}) async-start(), calls=%async_computation.2 | async-start | bytes 6963200 | tf_op jit(solution)/shard_map/all_gather | solution.py:17
  9.9 449.2 %reduce-scatter.2.cloned.1.call-start = ((), (), s32[]{:S(2)}) async-start(), calls=%async_computation.4 | async-start | bytes 2703360 | tf_op jit(solution)/shard_map/reduce_scatter | solution.py:25
  10.0 216.2 %copy-start.2 = (bf16[256,640]{1,0:T(8,128)(2,1)S(1)}, bf16[256,640]{1,0:T(8,128)(2,1)}, u32[]{:S(2)}) copy-start(bf16[256,640]{1,0:T(8,128)(2,1)} %param.10) | copy-start | bytes 983044
  237.9 36.7 %all-to-all-start = ((bf16[16,320,128]{2,1,0:T(8,128)(2,1)}), bf16[16,320,128]{2,1,0:T(8,128)(2,1)S(1)}, u32[]{:S(2)}, u32[]{:S(2)}) async-start(bf16[16,320,128]{2,1,0:T(8,128)(2,1)} %bitcast.28), calls=%async_computation | async-start | bytes 2621440 | tf_op jit(solution)/shard_map/while/body/eval_jaxpr/all_to_all | solution.py:37
  280.5 37.2 %all-to-all-start = ((bf16[16,320,128]{2,1,0:T(8,128)(2,1)}), bf16[16,320,128]{2,1,0:T(8,128)(2,1)S(1)}, u32[]{:S(2)}, u32[]{:S(2)}) async-start(bf16[16,320,128]{2,1,0:T(8,128)(2,1)} %bitcast.28), calls=%async_computation | async-start | bytes 2621440 | tf_op jit(solution)/shard_map/while/body/eval_jaxpr/all_to_all | solution.py:37
  323.5 37.5 %all-to-all-start = ((bf16[16,320,128]{2,1,0:T(8,128)(2,1)}), bf16[16,320,128]{2,1,0:T(8,128)(2,1)S(1)}, u32[]{:S(2)}, u32[]{:S(2)}) async-start(bf16[16,320,128]{2,1,0:T(8,128)(2,1)} %bitcast.28), calls=%async_computation | async-start | bytes 2621440 | tf_op jit(solution)/shard_map/while/body/eval_jaxpr/all_to_all | solution.py:37
  366.9 37.3 %all-to-all-start = ((bf16[16,320,128]{2,1,0:T(8,128)(2,1)}), bf16[16,320,128]{2,1,0:T(8,128)(2,1)S(1)}, u32[]{:S(2)}, u32[]{:S(2)}) async-start(bf16[16,320,128]{2,1,0:T(8,128)(2,1)} %bitcast.28), calls=%async_computation | async-start | bytes 2621440 | tf_op jit(solution)/shard_map/while/body/eval_jaxpr/all_to_all | solution.py:37
  410.0 37.3 %all-to-all-start = ((bf16[16,320,128]{2,1,0:T(8,128)(2,1)}), bf16[16,320,128]{2,1,0:T(8,128)(2,1)S(1)}, u32[]{:S(2)}, u32[]{:S(2)}) async-start(bf16[16,320,128]{2,1,0:T(8,128)(2,1)} %bitcast.28), calls=%async_computation | async-start | bytes 2621440 | tf_op jit(solution)/shard_map/while/body/eval_jaxpr/all_to_all | solution.py:37
  448.1 5.3 %copy-start = (bf16[256,5120]{0,1:T(8,128)(2,1)S(1)}, bf16[256,5120]{0,1:T(8,128)(2,1)}, u32[]{:S(2)}) copy-start(bf16[256,5120]{0,1:T(8,128)(2,1)} %all-gather.5.cloned.1.call-done) | copy-start | bytes 7864324
Sparse Core Ops, SparseCore 0:
  11.1 67.7 all-gather.4
  81.0 145.1 all-gather.2
  233.0 111.6 reduce-scatter.1
where the time goes:
time: 470 us; the launch traced here: 466 us
  waiting for transfers between devices  362 us (77%)
  starting transfers between devices  36.7 us (8%)
  local copies, waits for them, and re-layouts  23.7 us (5%)
  matrix products  22.8 us (5%)
  between operations  13.8 us (3%)
    all_to_all x5, waiting for transfers between devices, grad_block(): lax.all_to_all(partial_term, 'node', split_axis=0, concat_axis=0, tiled=T...  149 us
    all_gather x1, waiting for transfers between devices, on_device(): piece = lax.all_gather(weight_own, 'node', axis=0, tiled=True)  143 us
    all_gather x1, waiting for transfers between devices, on_device(): features = lax.all_gather(tokens, 'cross', axis=1, tiled=True)  68.9 us
    all_to_all x5, starting transfers between devices, grad_block(): lax.all_to_all(partial_term, 'node', split_axis=0, concat_axis=0, tiled=T...  36.6 us
    dot_general x5, matrix products, grad_block(): lax.dot_general(features, cot_columns, (((0,), (0,)), ((), ())), preferre...  11.4 us
  transfers between devices with their start and end apart: 8, of which 7 were waited for; matrix products, arithmetic and copies ran while one was open for 9% of the time, Pallas kernels for 0%

commit v1 on v0

v1 whole, which is shorter than its diff:
```python
import jax
import jax.numpy as jnp
from jax import lax
from jax.experimental import pallas as pl
from jax.experimental.pallas import tpu as pltpu
from jax.sharding import PartitionSpec as P

QBLOCK = 128
NY, NZ, NX = 8, 4, 4
MESH = pl.DeviceIdType.MESH
F32, BF16 = jnp.float32, jnp.bfloat16


def kernel(
    tok_ref, code_ref, scale_ref, cot_ref, exp_ref,
    out_ref, tgrad_ref, wgrad_ref,
    wts, cot, feats, pad, piece, part, from_core, summed, from_x, reduced, from_z,
    final, home, prod, ring, wg_send, wg_recv,
    cot_s, cot_r, one_s, one_r, tz_s, tz_r, tx_s, tx_r, tk_s, tk_r,
    gk_s, gk_r, gx_s, gx_r, gz_s, gz_r, ring_s, ring_r,
):
    node, cross = lax.axis_index("node"), lax.axis_index("cross")
    y, zl = node // 2, node % 2
    zh, x, k = cross // 8, (cross // 2) % NX, cross % 2
    tokens, width = cot_ref.shape
    half = tokens // 2
    rows = code_ref.shape[0]
    own = tok_ref.shape[1]

    def at(y=y, zl=zl, zh=zh, x=x, k=k):
        return (y * 2 + zl, zh * 8 + x * 2 + k)

    up, down = at(y=(y + 1) % NY), at(y=(y + NY - 1) % NY)
    pair = at(zl=1 - zl)
    core = at(k=1 - k)
    zs = [at(zh=(zh + o) % NZ) for o in range(1, NZ)]
    xs = [at(x=(x + o) % NX) for o in range(1, NX)]
    held = 2 * zh + x // 2
    swap = at(y=held, zh=y // 2, x=2 * (y % 2) + x % 2)
    away = held != y

    def remote(src, dst, send, recv, device):
        return pltpu.make_async_remote_copy(
            src_ref=src, dst_ref=dst, send_sem=send, recv_sem=recv,
            device_id=device, device_id_type=MESH,
        )

    started = []

    def go(copy):
        copy.start()
        started.append(copy)

    own_rows = pl.ds(pl.multiple_of(zl * rows, 32), rows)
    other_rows = pl.ds(pl.multiple_of((1 - zl) * rows, 32), rows)
    pad[...] = jnp.zeros_like(pad)
    pad[:, :own] = tok_ref[...]
    piece[...] = pad[...].T[:own]
    for b in range(width // QBLOCK):
        cols = slice(b * QBLOCK, (b + 1) * QBLOCK)
        wts[own_rows, cols] = (
            code_ref[:, cols].astype(F32) * scale_ref[:, b : b + 1]
        ).astype(BF16)

    barrier = pltpu.get_barrier_semaphore()
    friends = [up, down, pair, core] + zs + xs
    for device in friends:
        pl.semaphore_signal(barrier, inc=1, device_id=device, device_id_type=MESH)

    @pl.when(away)
    def _():
        pl.semaphore_signal(barrier, inc=1, device_id=swap, device_id_type=MESH)

    pl.semaphore_wait(barrier, len(friends) + away.astype(jnp.int32))

    def spot(t, g):
        return feats.at[t, pl.ds(pl.multiple_of(g * own, 32), own)]

    held_g = 2 * (x % 2) + k
    to_held = remote(piece, spot(y, held_g), one_s.at[0], one_r.at[0], swap)

    @pl.when(away)
    def _():
        to_held.start()

    wsend = remote(wts.at[own_rows], wts.at[own_rows], one_s.at[1], one_r.at[1], pair)
    go(wsend)

    hs = [pl.ds(0, half), pl.ds(half, half)]
    ways = [(up, -1), (down, 1)]

    def cot_copy(way, h, s, first):
        device, sign = ways[way]
        t = (y + sign * s + NY) % NY
        src = cot_ref.at[hs[h]] if first else cot.at[t, hs[h]]
        return remote(src, cot.at[t, hs[h]], cot_s.at[way, h, s], cot_r.at[way, h, s], device)

    def cot_arrive(way, h, s):
        t = (y + ways[way][1] * (s + 1) + NY) % NY
        slot = cot.at[t, hs[h]]
        remote(slot, slot, cot_s.at[way, h, s], cot_r.at[way, h, s], up).wait_recv()

    for i in range(2):
        for way in range(2):
            go(cot_copy(way, (i + way) % 2, 0, True))
    cot[y] = cot_ref[...]

    def cot_step(i):
        s = i // 2
        for way in range(2):
            h = (i + way) % 2
            cot_arrive(way, h, s)
            if i < 5:
                go(cot_copy(way, h, s + 1, False))

    def dist(i):
        return (y + i + NY) % NY

    def tok_send_x(a):
        t = 2 * ((zh + a) % NZ) + x // 2
        for o in range(1, NX):
            go(remote(spot(t, held_g), spot(t, held_g), tx_s.at[a, o - 1], tx_r.at[a, o - 1], xs[o - 1]))

    def tok_send_core(t, xl):
        g = 2 * xl + k
        go(remote(spot(t, g), spot(t, g), tk_s.at[t, xl], tk_r.at[t, xl], core))

    def tok_held():
        @pl.when(away)
        def _():
            slot = spot(held, held_g)
            remote(slot, slot, one_s.at[0], one_r.at[0], swap).wait_recv()

        @pl.when(jnp.logical_not(away))
        def _():
            spot(held, held_g)[...] = piece[...]

        for o in range(1, NZ):
            go(remote(spot(held, held_g), spot(held, held_g), tz_s.at[o - 1], tz_r.at[o - 1], zs[o - 1]))
        tok_send_x(0)
        tok_send_core(held, x % 2)

    def tok_from_z(a):
        t = 2 * ((zh + a) % NZ) + x // 2
        slot = spot(t, held_g)
        remote(slot, slot, tz_s.at[NZ - a - 1], tz_r.at[NZ - a - 1], core).wait_recv()
        tok_send_x(a)
        tok_send_core(t, x % 2)

    def tok_from_x(a, o):
        there = (x + o) % NX
        t = 2 * ((zh + a) % NZ) + there // 2
        slot = spot(t, 2 * (there % 2) + k)
        remote(slot, slot, tx_s.at[a, NX - o - 1], tx_r.at[a, NX - o - 1], core).wait_recv()
        tok_send_core(t, there % 2)

    def tok_from_core():
        for t in range(NY):
            for xl in range(2):
                slot = spot(t, 2 * xl + 1 - k)
                remote(slot, slot, tk_s.at[t, xl], tk_r.at[t, xl], core).wait_recv()

    def tg_part(t):
        part[t] = lax.dot_general(
            wts[...], cot[t], (((1,), (1,)), ((), ())), preferred_element_type=F32
        ).astype(BF16)
        for xl in range(2):
            src = part.at[t, pl.ds(pl.multiple_of((2 * xl + 1 - k) * own, 32), own)]
            go(remote(src, from_core.at[t, xl], gk_s.at[t, xl], gk_r.at[t, xl], core))

    def tg_x_copy(t, xl):
        there = 2 * (t % 2) + xl
        o = (x - there + NX) % NX
        slot = lax.max(o - 1, 0)
        return there != x, remote(
            summed.at[t, xl], from_x.at[t // 2, slot], gx_s.at[t, xl],
            gx_r.at[t // 2, slot], at(x=there),
        )

    def tg_sum(t):
        for xl in range(2):
            slot = from_core.at[t, xl]
            remote(slot, slot, gk_s.at[t, xl], gk_r.at[t, xl], core).wait_recv()
            mine = part[t, pl.ds(pl.multiple_of((2 * xl + k) * own, 32), own)]
            summed[t, xl] = (mine.astype(F32) + slot[...].astype(F32)).astype(BF16)
            leaves, copy = tg_x_copy(t, xl)

            @pl.when(leaves)
            def _():
                copy.start()

    def tg_from_x(a):
        b = (zh + a) % NZ
        total = summed[2 * b + x // 2, x % 2].astype(F32)
        for o in range(NX - 1):
            slot = from_x.at[b, o]
            remote(slot, slot, gx_s.at[0, 0], gx_r.at[b, o], core).wait_recv()
            total += slot[...].astype(F32)
        reduced[a] = total.astype(BF16)
        if a:
            go(remote(reduced.at[a], from_z.at[a - 1], gz_s.at[a - 1], gz_r.at[a - 1], zs[a - 1]))

    tg_home = remote(final, home, one_s.at[2], one_r.at[2], swap)

    def tg_from_z():
        total = reduced[0].astype(F32)
        for o in range(NZ - 1):
            slot = from_z.at[o]
            remote(slot, slot, gz_s.at[o], gz_r.at[o], core).wait_recv()
            total += slot[...].astype(F32)
        final[...] = total.astype(BF16)

        @pl.when(away)
        def _():
            tg_home.start()

    def tg_end():
        @pl.when(away)
        def _():
            tg_home.wait_recv()

        @pl.when(jnp.logical_not(away))
        def _():
            home[...] = final[...]

        pad[:own] = home[...]
        tgrad_ref[...] = pad[...].T[:, :own]

    def product(t):
        prod[t] = lax.dot_general(
            feats[t], wts[...], (((0,), (0,)), ((), ())), preferred_element_type=F32
        )

    def ring_copy(way, i):
        s, h = i // 2, (i + way) % 2
        return remote(
            ring.at[way, i], ring.at[way, i + 2], ring_s.at[way, i], ring_r.at[way, i], ways[way][0]
        )

    def ring_goal(way, i):
        steps = (4 if i % 2 == 0 else 3) - i // 2
        return (y - ways[way][1] * steps + NY) % NY

    def ring_start(way, i):
        h = (i + way) % 2
        ring[way, i] = prod[ring_goal(way, i), hs[h]].astype(BF16)
        go(ring_copy(way, i))

    def ring_step(i):
        for way in range(2):
            h = (i + way) % 2
            slot = ring.at[way, i + 2]
            remote(slot, slot, ring_s.at[way, i], ring_r.at[way, i], core).wait_recv()
            if i < 5:
                slot[...] = (
                    slot[...].astype(F32) + prod[ring_goal(way, i + 2), hs[h]]
                ).astype(BF16)
                go(ring_copy(way, i + 2))

    def wg_half(which):
        total = jnp.zeros((rows, width), F32)
        for t in range(NY):
            total += jnp.dot(feats[t, which], cot[t], preferred_element_type=F32)
        return total

    wg_copy = remote(wg_send, wg_recv, one_s.at[3], one_r.at[3], pair)

    def wg_start():
        wg_send[...] = wg_half(other_rows).astype(BF16)
        go(wg_copy)

    def wg_own():
        wgrad_ref[...] = wg_half(own_rows)

    def wg_end():
        wg_copy.wait_recv()
        factor = jnp.exp2(-exp_ref[...].astype(F32))
        for b in range(width // QBLOCK):
            cols = slice(b * QBLOCK, (b + 1) * QBLOCK)
            wgrad_ref[:, cols] = (
                wgrad_ref[:, cols] + wg_recv[:, cols].astype(F32)
            ) * factor[:, b : b + 1]

    cot_step(0)
    tok_held()
    cot_step(1)
    remote(wts.at[other_rows], wts.at[other_rows], one_s.at[1], one_r.at[1], pair).wait_recv()
    for i in (0, 1, -1):
        tg_part(dist(i))
    for a in (1, 3, 2):
        tok_from_z(a)
    cot_step(2)
    for o in (1, 3, 2):
        tok_from_x(0, o)
    for i in (0, 1, -1):
        tg_sum(dist(i))
    cot_step(3)
    for i in (2, -2):
        tg_part(dist(i))
    for o in (1, 3, 2):
        tok_from_x(1, o)
    cot_step(4)
    for i in (2, -2):
        tg_sum(dist(i))
    for a in (3, 2):
        for o in (1, 3, 2):
            tok_from_x(a, o)
    cot_step(5)
    tok_from_core()
    product(dist(4))
    ring_start(0, 0)
    ring_start(1, 0)
    product(dist(3))
    ring_start(0, 1)
    product(dist(-3))
    ring_start(1, 1)
    for i in (3, -3):
        tg_part(dist(i))
    product(dist(2))
    product(dist(-2))
    cot_step(6)
    tg_part(dist(4))
    for i in (3, -3):
        tg_sum(dist(i))
    ring_step(0)
    tg_sum(dist(4))
    product(dist(1))
    product(dist(-1))
    ring_step(1)
    wg_start()
    ring_step(2)
    for a in (1, 2, 3, 0):
        tg_from_x(a)
    product(y)
    ring_step(3)
    wg_own()
    tg_from_z()
    ring_step(4)
    tg_end()
    wg_end()
    ring_step(5)
    ring_step(6)
    for h in range(2):
        out_ref[hs[h]] = (
            prod[y, hs[h]]
            + ring[0, 8 - h].astype(F32)
            + ring[1, 7 + h].astype(F32)
        ).astype(BF16)

    for copy in started:
        copy.wait_send()
    for t in range(NY):
        for xl in range(2):
            leaves, copy = tg_x_copy(t, xl)

            @pl.when(leaves)
            def _():
                copy.wait_send()

    @pl.when(away)
    def _():
        to_held.wait_send()
        tg_home.wait_send()


def on_device(tokens, weight_codes, weight_scales, cotangent, grad_exponents):
    count, own = tokens.shape
    rows, width = weight_codes.shape
    depth = 2 * rows
    dma = pltpu.SemaphoreType.DMA
    vmem = pl.BlockSpec(memory_space=pltpu.VMEM)
    scratch = [
        pltpu.VMEM((depth, width), BF16),
        pltpu.VMEM((NY, count, width), BF16),
        pltpu.VMEM((NY, depth, count), BF16),
        pltpu.VMEM((count, count), BF16),
        pltpu.VMEM((own, count), BF16),
        pltpu.VMEM((NY, depth, count), BF16),
        pltpu.VMEM((NY, 2, own, count), BF16),
        pltpu.VMEM((NY, 2, own, count), BF16),
        pltpu.VMEM((NZ, NX - 1, own, count), BF16),
        pltpu.VMEM((NZ, own, count), BF16),
        pltpu.VMEM((NZ - 1, own, count), BF16),
        pltpu.VMEM((own, count), BF16),
        pltpu.VMEM((own, count), BF16),
        pltpu.VMEM((NY, count, width), F32),
        pltpu.VMEM((2, 9, count // 2, width), BF16),
        pltpu.VMEM((rows, width), BF16),
        pltpu.VMEM((rows, width), BF16),
        dma((2, 2, 4)), dma((2, 2, 4)),
        dma((4,)), dma((4,)),
        dma((NZ - 1,)), dma((NZ - 1,)),
        dma((NZ, NX - 1)), dma((NZ, NX - 1)),
        dma((NY, 2)), dma((NY, 2)),
        dma((NY, 2)), dma((NY, 2)),
        dma((NY, 2)), dma((NZ, NX - 1)),
        dma((NZ - 1,)), dma((NZ - 1,)),
        dma((2, 7)), dma((2, 7)),
    ]
    return pl.pallas_call(
        kernel,
        name="up_projection",
        out_shape=(
            jax.ShapeDtypeStruct((count, width), BF16),
            jax.ShapeDtypeStruct((count, own), BF16),
            jax.ShapeDtypeStruct((rows, width), F32),
        ),
        in_specs=[vmem] * 5,
        out_specs=(vmem, vmem, vmem),
        scratch_shapes=scratch,
        compiler_params=pltpu.CompilerParams(
            collective_id=0, has_side_effects=True, vmem_limit_bytes=56 << 20
        ),
    )(tokens, weight_codes, weight_scales, cotangent, grad_exponents)


def solution(mesh):
    placed = P("node", "cross")
    return jax.shard_map(
        on_device,
        mesh=mesh,
        in_specs=(placed,) * 5,
        out_specs=(placed,) * 3,
        check_vma=False,
    )
```

time: 470 us -> 110 us (0.23)
  the two profiles are of different devices: /device:TPU:1 before, /device:TPU:86 now
where the time goes in v1:
time: 110 us
  Pallas kernels  101 us (92%)
  local copies, waits for them, and re-layouts  7.63 us (7%)
    pallas_call x1, Pallas kernels, on_device(): pl.pallas_call(kernel, name='up_projection', out_shape=(jax.ShapeDtypeStr...  101 us
    unnamed x11, local copies, waits for them, and re-layouts  5.91 us

profile of v1, /device:TPU:86, one launch (start us, length us, event | category | flops | bytes accessed | tf_op | source)
XLA Modules:
  0.0 109.5 jit_solution(12737612916579930840)
XLA Ops:
  0.6 0.0 copy-start.1
  0.6 1.7 %copy.8.tok_ref = bf16[256,160]{1,0:T(8,128)(2,1)} copy(bf16[256,160]{0,1:T(8,128)(2,1)} %param.5) | data formatting | bytes 163840 | tf_op args[0]
  2.3 0.0 copy-done.1
  2.3 0.0 copy-start.2
  2.3 0.8 copy.9.scale_ref
  3.1 0.0 copy-done.2
  3.1 0.8 copy.10.exp_ref
  3.9 101.2 %up_projection.1 = (bf16[256,640]{1,0:T(8,128)(2,1)}, bf16[256,160]{1,0:T(8,128)(2,1)}, f32[320,640]{1,0:T(8,128)}) custom-call(bf16[256,160]{1,0:T(8,128)(2,1)} %copy.8.tok_ref, s32[320,640]{1,0:T(8,128)} %code_ref.1, f32[320,5]{1,0:T(8,128)} %copy.9.scale_ref, bf16[256,640]{1,0:T(8,128)(2,1)} %cot_ref.1, s32[320,5]{1,0:T(8,128)} %copy.10.exp_ref), custom_call_target="tpu_custom_call" | custom-call | tf_op jit(solution)/shard_map/up_projection/pallas_call | solution.py:400
  105.2 0.0 copy-start
  105.2 1.7 %copy.11 = bf16[256,160]{0,1:T(8,128)(2,1)} copy(bf16[256,160]{1,0:T(8,128)(2,1)} %get-tuple-element.4) | data formatting | bytes 163840 | tf_op jit(solution)/shard_map/up_projection/pallas_call | solution.py:400
  106.9 1.7 %copy.14 = bf16[256,640]{1,0:T(8,128)(2,1)} copy(bf16[256,640]{1,0:T(8,128)(2,1)} %get-tuple-element.9) | data formatting | bytes 655360
  108.6 0.0 copy-done
  108.6 0.9 copy.15
Async XLA Ops:
  0.6 1.7 %copy-start.1 = (f32[320,5]{0,1:T(8,128)S(1)}, f32[320,5]{0,1:T(8,128)}, u32[]{:S(2)}) copy-start(f32[320,5]{0,1:T(8,128)} %param.7) | copy-start | bytes 19204
  2.3 0.8 copy-start.2
  105.2 3.5 %copy-start = (f32[320,640]{1,0:T(8,128)S(1)}, f32[320,640]{1,0:T(8,128)}, u32[]{:S(2)}) copy-start(f32[320,640]{1,0:T(8,128)} %get-tuple-element.11) | copy-start | bytes 2457604

commit v2 on v1

v2 whole, which is shorter than its diff:
```python
import jax
import jax.numpy as jnp
from jax import lax
from jax.experimental import pallas as pl
from jax.experimental.pallas import tpu as pltpu
from jax.sharding import PartitionSpec as P

QBLOCK = 128
VMEM = 40 << 20
NY, NZ, NX = 8, 4, 4
HERE = NY // 2
PARTS = 2
MESH = pl.DeviceIdType.MESH
F32, BF16 = jnp.float32, jnp.bfloat16


def kernel(
    tok_hbm, code_hbm, scale_hbm, cot_hbm, exp_hbm,
    out_ref, tgrad_ref, wgrad_ref,
    tok, code, scale, expo, wts, cot, feats, narrow, part, from_core, summed,
    from_x, reduced, from_z, final, home, prod, ring, wg_send, wg_recv,
    in_s, to_s, to_r, cot_s, cot_r, one_s, one_r, tz_s, tz_r, tx_s, tx_r, tk_s, tk_r,
    gk_s, gk_r, gx_s, gx_r, gz_s, gz_r, ring_s, ring_r,
):
    node, cross = lax.axis_index("node"), lax.axis_index("cross")
    y, zl = node // 2, node % 2
    zh, x, k = cross // 8, (cross // 2) % NX, cross % 2
    tokens, width = cot_hbm.shape
    half = tokens // 2
    rows = code_hbm.shape[0]
    own = tok_hbm.shape[0]

    own_slot = cot.at[HERE]
    loads = [
        pltpu.make_async_copy(src, dst, in_s.at[i])
        for i, (src, dst) in enumerate(
            [(tok_hbm, tok), (cot_hbm, own_slot), (code_hbm, code), (scale_hbm, scale), (exp_hbm, expo)]
        )
    ]
    for load in loads:
        load.start()

    def at(y=y, zl=zl, zh=zh, x=x, k=k):
        return (y * 2 + zl, zh * 8 + x * 2 + k)

    up, down = at(y=(y + 1) % NY), at(y=(y + NY - 1) % NY)
    pair = at(zl=1 - zl)
    core = at(k=1 - k)
    zs = [at(zh=(zh + o) % NZ) for o in range(1, NZ)]
    xs = [at(x=(x + o) % NX) for o in range(1, NX)]
    place = 2 * zh + x // 2
    slot_there = (y - place + HERE + NY) % NY
    owner = at(y=place, zh=slot_there // 2, x=2 * (slot_there % 2) + x % 2)
    home_of = at(y=(y + NY - HERE + place) % NY, zh=y // 2, x=2 * (y % 2) + x % 2)
    moves = jnp.logical_or(place != y, place != HERE)

    def remote(src, dst, send, recv, device):
        return pltpu.make_async_remote_copy(
            src_ref=src, dst_ref=dst, send_sem=send, recv_sem=recv,
            device_id=device, device_id_type=MESH,
        )

    def landed(slot, recv):
        remote(slot, slot, one_s.at[0], recv, core).wait_recv()

    started = []

    def go(copy):
        copy.start()
        started.append(copy)

    def columns(blocks):
        count = blocks.shape[0]
        narrow[...] = jnp.zeros_like(narrow)
        narrow[:count, :rows] = blocks
        return narrow[...].T[:rows, :count]

    barrier = pltpu.get_barrier_semaphore()
    friends = [up, down, pair, core] + zs + xs

    def greet(device):
        pl.semaphore_signal(barrier, inc=1, device_id=device, device_id_type=MESH)

    for device in friends:
        greet(device)

    @pl.when(moves)
    def _():
        greet(owner)
        greet(home_of)

    pl.semaphore_wait(barrier, len(friends) + 2 * moves.astype(jnp.int32))

    size = own // PARTS

    def spot(e, g, p=None):
        start = g * own if p is None else g * own + p * size
        return feats.at[e, pl.ds(pl.multiple_of(start, 16), own if p is None else size)]

    own_g = 2 * (x % 2) + k
    to_owner = [
        remote(tok.at[pl.ds(p * size, size)], spot(slot_there, own_g, p), to_s.at[p], to_r.at[p], owner)
        for p in range(PARTS)
    ]

    def tok_start():
        @pl.when(moves)
        def _():
            for copy in to_owner:
                copy.start()

        @pl.when(jnp.logical_not(moves))
        def _():
            spot(place, own_g)[...] = tok[...]

    def tok_send_x(j, p):
        src = spot(2 * j + x // 2, own_g, p)
        for o in (1, 3, 2):
            go(remote(src, src, tx_s.at[j, o - 1, p], tx_r.at[j, o - 1, p], xs[o - 1]))

    def tok_send_core(e, xl):
        src = spot(e, 2 * xl + k)
        go(remote(src, src, tk_s.at[e, xl], tk_r.at[e, xl], core))

    def tok_own():
        for p in range(PARTS):
            src = spot(place, own_g, p)

            @pl.when(moves)
            def _():
                landed(src, to_r.at[p])

            for o in range(1, NZ):
                go(remote(src, src, tz_s.at[o - 1, p], tz_r.at[zh, p], zs[o - 1]))
            tok_send_x(zh, p)
        tok_send_core(place, x % 2)

    need = [0, 3, 1, 2]
    ahead = (zh > 0).astype(jnp.int32) + (zh % 3 > 0).astype(jnp.int32) + (zh == 2).astype(jnp.int32)
    turn_of = [zh]
    for m in range(NZ - 1):
        later = (ahead <= m).astype(jnp.int32)
        turn_of.append(need[m] + later * (need[m + 1] - need[m]))

    def tok_from_z(m):
        j = turn_of[m]
        e = 2 * j + x // 2
        for p in range(PARTS):
            landed(spot(e, own_g, p), tz_r.at[j, p])
            tok_send_x(j, p)
        tok_send_core(e, x % 2)

    def tok_from_x(m):
        j = turn_of[m]
        for o in (1, 3, 2):
            there = (x + o) % NX
            e = 2 * j + there // 2
            for p in range(PARTS):
                landed(spot(e, 2 * (there % 2) + k, p), tx_r.at[j, NX - o - 1, p])
            tok_send_core(e, there % 2)

    def tok_from_core(e):
        for xl in range(2):
            landed(spot(e, 2 * xl + 1 - k), tk_r.at[e, xl])

    own_rows = pl.ds(pl.multiple_of(zl * rows, 32), rows)
    other_rows = pl.ds(pl.multiple_of((1 - zl) * rows, 32), rows)
    wsend = remote(wts.at[own_rows], wts.at[own_rows], one_s.at[1], one_r.at[1], pair)

    def weights_own():
        loads[2].wait()
        loads[3].wait()
        scales = columns(scale[...])
        for b in range(width // QBLOCK):
            cols = slice(b * QBLOCK, (b + 1) * QBLOCK)
            wts[own_rows, cols] = (
                code[:, cols].astype(F32) * scales[:, b : b + 1]
            ).astype(BF16)

    def weights_send():
        go(wsend)

    def weights_other():
        landed(wts.at[other_rows], one_r.at[1])

    hs = [pl.ds(0, half), pl.ds(half, half)]
    ways = [(up, -1), (down, 1)]

    def cot_slot(way, s):
        return (HERE + ways[way][1] * s + NY) % NY

    def cot_copy(way, h, s):
        return remote(
            cot.at[cot_slot(way, s), hs[h]], cot.at[cot_slot(way, s + 1), hs[h]],
            cot_s.at[way, h, s], cot_r.at[way, h, s], ways[way][0],
        )

    def cot_start():
        for i in range(2):
            for way in range(2):
                go(cot_copy(way, (i + way) % 2, 0))

    def cot_step(i):
        s = i // 2
        for way in range(2):
            h = (i + way) % 2
            landed(cot.at[cot_slot(way, s + 1), hs[h]], cot_r.at[way, h, s])
            if i < 5:
                go(cot_copy(way, h, s + 1))

    def tg_part(i):
        e = (HERE + i) % NY
        part[e] = lax.dot_general(
            wts[...], cot[e], (((1,), (1,)), ((), ())), preferred_element_type=F32
        ).astype(BF16)
        for xl in range(2):
            src = part.at[e, pl.ds(pl.multiple_of((2 * xl + 1 - k) * own, 32), own)]
            go(remote(src, from_core.at[e, xl], gk_s.at[e, xl], gk_r.at[e, xl], core))

    def tg_x_copy(e, xl):
        there = 2 * (e % 2) + xl
        o = (x - there + NX) % NX
        slot = lax.max(o - 1, 0)
        return there != x, remote(
            summed.at[e, xl], from_x.at[e // 2, slot], gx_s.at[e, xl],
            gx_r.at[e // 2, slot], at(x=there),
        )

    def tg_sum(i):
        e = (HERE + i) % NY
        for xl in range(2):
            slot = from_core.at[e, xl]
            landed(slot, gk_r.at[e, xl])
            mine = part[e, pl.ds(pl.multiple_of((2 * xl + k) * own, 32), own)]
            summed[e, xl] = (mine.astype(F32) + slot[...].astype(F32)).astype(BF16)
            leaves, copy = tg_x_copy(e, xl)

            @pl.when(leaves)
            def _():
                copy.start()

    def tg_z_copy(j):
        o = (zh - j + NZ) % NZ
        slot = lax.max(o - 1, 0)
        return j != zh, remote(
            reduced.at[j], from_z.at[slot], gz_s.at[j], gz_r.at[slot], at(zh=j)
        )

    def tg_from_x(j):
        total = summed[2 * j + x // 2, x % 2].astype(F32)
        for o in range(NX - 1):
            landed(from_x.at[j, o], gx_r.at[j, o])
            total += from_x[j, o].astype(F32)
        reduced[j] = total.astype(BF16)
        leaves, copy = tg_z_copy(j)

        @pl.when(leaves)
        def _():
            copy.start()

    to_home = remote(final, home, one_s.at[2], one_r.at[2], home_of)

    def tg_from_z():
        total = reduced[zh].astype(F32)
        for o in range(NZ - 1):
            landed(from_z.at[o], gz_r.at[o])
            total += from_z[o].astype(F32)
        final[...] = total.astype(BF16)

        @pl.when(moves)
        def _():
            to_home.start()

    def tg_end():
        @pl.when(moves)
        def _():
            to_home.wait_recv()
            tgrad_ref[...] = home[...]

        @pl.when(jnp.logical_not(moves))
        def _():
            tgrad_ref[...] = final[...]

    def product(i):
        e = (HERE + i) % NY
        prod[e] = lax.dot_general(
            feats[e], wts[...], (((0,), (0,)), ((), ())), preferred_element_type=F32
        )

    def ring_copy(way, i):
        return remote(
            ring.at[way, i], ring.at[way, i + 2], ring_s.at[way, i], ring_r.at[way, i], ways[way][0]
        )

    def ring_goal(way, i):
        steps = (4 if i % 2 == 0 else 3) - i // 2
        return (HERE - ways[way][1] * steps + NY) % NY

    def ring_start(way, i):
        h = (i + way) % 2
        ring[way, i] = prod[ring_goal(way, i), hs[h]].astype(BF16)
        go(ring_copy(way, i))

    def ring_step(i):
        for way in range(2):
            h = (i + way) % 2
            slot = ring.at[way, i + 2]
            landed(slot, ring_r.at[way, i])
            if i < 5:
                slot[...] = (
                    slot[...].astype(F32) + prod[ring_goal(way, i + 2), hs[h]]
                ).astype(BF16)
                go(ring_copy(way, i + 2))

    def wg_half(which):
        total = jnp.zeros((rows, width), F32)
        for e in range(NY):
            total += jnp.dot(feats[e, which], cot[e], preferred_element_type=F32)
        return total

    wg_copy = remote(wg_send, wg_recv, one_s.at[3], one_r.at[3], pair)

    def wg_start():
        wg_send[...] = wg_half(other_rows).astype(BF16)
        go(wg_copy)

    def wg_own():
        wgrad_ref[...] = wg_half(own_rows)

    def wg_end():
        wg_copy.wait_recv()
        factor = columns(jnp.exp2(-expo[...].astype(F32)))
        for b in range(width // QBLOCK):
            cols = slice(b * QBLOCK, (b + 1) * QBLOCK)
            wgrad_ref[:, cols] = (
                wgrad_ref[:, cols] + wg_recv[:, cols].astype(F32)
            ) * factor[:, b : b + 1]

    loads[0].wait()
    tok_start()
    loads[1].wait()
    cot_start()
    weights_own()
    weights_send()
    loads[4].wait()
    cot_step(0)
    tok_own()
    cot_step(1)
    tok_from_z(1)
    cot_step(2)
    tok_from_z(2)
    tok_from_x(0)
    tok_from_z(3)
    cot_step(3)
    weights_other()
    for i in (0, 1, -1):
        tg_part(i)
    tok_from_x(1)
    for i in (0, 1, -1):
        tg_sum(i)
    cot_step(4)
    for i in (2, -2):
        tg_part(i)
    tok_from_x(2)
    for e in (0, 1, 7):
        tok_from_core(e)
    product(4)
    ring_start(0, 0)
    ring_start(1, 0)
    product(3)
    ring_start(0, 1)
    product(-3)
    ring_start(1, 1)
    tok_from_x(3)
    for i in (2, -2):
        tg_sum(i)
    cot_step(5)
    for i in (3, -3):
        tg_part(i)
    cot_step(6)
    tg_part(4)
    for e in (6, 2):
        tok_from_core(e)
    product(2)
    product(-2)
    for i in (3, -3, 4):
        tg_sum(i)
    ring_step(0)
    for e in (5, 3, 4):
        tok_from_core(e)
    wg_start()
    tg_from_x(2)
    ring_step(1)
    product(1)
    product(-1)
    tg_from_x(1)
    tg_from_x(3)
    ring_step(2)
    tg_from_x(0)
    product(0)
    ring_step(3)
    tg_from_z()
    ring_step(4)
    wg_own()
    wg_end()
    ring_step(5)
    tg_end()
    ring_step(6)
    for h in range(2):
        out_ref[hs[h]] = (
            prod[HERE, hs[h]]
            + ring[0, 8 - h].astype(F32)
            + ring[1, 7 + h].astype(F32)
        ).astype(BF16)

    for copy in started:
        copy.wait_send()
    some = [tg_x_copy(e, xl) for e in range(NY) for xl in range(2)]
    some += [tg_z_copy(j) for j in range(NZ)]
    some += [(moves, copy) for copy in to_owner + [to_home]]
    for leaves, copy in some:

        @pl.when(leaves)
        def _():
            copy.wait_send()


def on_device(tokens, weight_codes, weight_scales, cotangent, grad_exponents):
    count, own = tokens.shape
    rows, width = weight_codes.shape
    depth = 2 * rows
    dma = pltpu.SemaphoreType.DMA
    vmem = pl.BlockSpec(memory_space=pltpu.VMEM)
    scratch = [
        pltpu.VMEM((own, count), BF16),
        pltpu.VMEM((rows, width), jnp.int32),
        pltpu.VMEM((width // QBLOCK, rows), F32),
        pltpu.VMEM((width // QBLOCK, rows), jnp.int32),
        pltpu.VMEM((depth, width), BF16),
        pltpu.VMEM((NY, count, width), BF16),
        pltpu.VMEM((NY, depth, count), BF16),
        pltpu.VMEM((8, -(-rows // 128) * 128), F32),
        pltpu.VMEM((NY, depth, count), BF16),
        pltpu.VMEM((NY, 2, own, count), BF16),
        pltpu.VMEM((NY, 2, own, count), BF16),
        pltpu.VMEM((NZ, NX - 1, own, count), BF16),
        pltpu.VMEM((NZ, own, count), BF16),
        pltpu.VMEM((NZ - 1, own, count), BF16),
        pltpu.VMEM((own, count), BF16),
        pltpu.VMEM((own, count), BF16),
        pltpu.VMEM((NY, count, width), F32),
        pltpu.VMEM((2, 9, count // 2, width), BF16),
        pltpu.VMEM((rows, width), BF16),
        pltpu.VMEM((rows, width), BF16),
        dma((5,)),
        dma((PARTS,)), dma((PARTS,)),
        dma((2, 2, 4)), dma((2, 2, 4)),
        dma((4,)), dma((4,)),
        dma((NZ - 1, PARTS)), dma((NZ, PARTS)),
        dma((NZ, NX - 1, PARTS)), dma((NZ, NX - 1, PARTS)),
        dma((NY, 2)), dma((NY, 2)),
        dma((NY, 2)), dma((NY, 2)),
        dma((NY, 2)), dma((NZ, NX - 1)),
        dma((NZ,)), dma((NZ - 1,)),
        dma((2, 7)), dma((2, 7)),
    ]
    projected, token_grad, weight_grad = pl.pallas_call(
        kernel,
        name="up_projection",
        out_shape=(
            jax.ShapeDtypeStruct((count, width), BF16),
            jax.ShapeDtypeStruct((own, count), BF16),
            jax.ShapeDtypeStruct((rows, width), F32),
        ),
        in_specs=[pl.BlockSpec(memory_space=pltpu.HBM)] * 5,
        out_specs=(vmem, vmem, vmem),
        scratch_shapes=scratch,
        compiler_params=pltpu.CompilerParams(
            collective_id=0, has_side_effects=True, vmem_limit_bytes=VMEM
        ),
    )(tokens.T, weight_codes, weight_scales.T, cotangent, grad_exponents.T)
    return projected, token_grad.T, weight_grad


def solution(mesh):
    placed = P("node", "cross")
    return jax.shard_map(
        on_device,
        mesh=mesh,
        in_specs=(placed,) * 5,
        out_specs=(placed,) * 3,
        check_vma=False,
    )
```

time: 110 us -> 94.9 us (0.86)
  the two profiles are of different devices: /device:TPU:86 before, /device:TPU:1 now
where the time goes in v2:
time: 94.9 us; the launch traced here: 94.6 us
  Pallas kernels  87.3 us (92%)
  local copies, waits for them, and re-layouts  6.66 us (7%)
    pallas_call x1, Pallas kernels, on_device(): pl.pallas_call(kernel, name='up_projection', out_shape=(jax.ShapeDtypeStr...  87.3 us
    unnamed x13, local copies, waits for them, and re-layouts  6.66 us

profile of v2, /device:TPU:1, one launch (start us, length us, event | category | flops | bytes accessed | tf_op | source)
XLA Modules:
  0.0 94.6 jit_solution(4307302593486212982)
XLA Ops:
  0.6 0.0 copy-start
  0.6 1.1 %copy-done = s32[320,640]{1,0:T(8,128)S(1)} copy-done((s32[320,640]{1,0:T(8,128)S(1)}, s32[320,640]{1,0:T(8,128)}, u32[]{:S(2)}) %copy-start) | copy-done | bytes 819224
  1.8 0.0 copy-start.1
  1.8 1.0 %copy-done.1 = bf16[256,640]{1,0:T(8,128)(2,1)S(1)} copy-done((bf16[256,640]{1,0:T(8,128)(2,1)S(1)}, bf16[256,640]{1,0:T(8,128)(2,1)}, u32[]{:S(2)}) %copy-start.1) | copy-done | bytes 327704
  2.8 0.0 copy-start.2
  2.8 0.9 copy-done.2
  3.6 0.0 copy-start.3
  3.6 0.7 copy-done.3
  4.3 0.0 copy-start.4
  4.3 0.7 copy-done.4
  5.1 87.3 %up_projection.1 = (bf16[256,640]{1,0:T(8,128)(2,1)S(1)}, bf16[160,256]{1,0:T(8,128)(2,1)S(1)}, f32[320,640]{1,0:T(8,128)S(1)}) custom-call(bf16[160,256]{1,0:T(8,128)(2,1)S(1)} %bitcast.4, s32[320,640]{1,0:T(8,128)S(1)} %copy-done, f32[5,320]{1,0:T(8,128)S(1)} %bitcast.6, bf16[256,640]{1,0:T(8,128)(2,1)S(1)} %copy-done.1, s32[5,320]{1,0:T(8,128)S(1)} %bitcast.7), custom_call_target="tpu_custom_call" | custom-call | tf_op jit(solution)/shard_map/up_projection/pallas_call | solution.py:467
  92.4 0.7 copy.11
  93.1 0.6 copy.12
  93.7 0.9 copy.13
Async XLA Ops:
  0.6 1.1 %copy-start = (s32[320,640]{1,0:T(8,128)S(1)}, s32[320,640]{1,0:T(8,128)}, u32[]{:S(2)}) copy-start(s32[320,640]{1,0:T(8,128)} %code_hbm.1) | copy-start | bytes 2457604
  1.8 1.0 %copy-start.1 = (bf16[256,640]{1,0:T(8,128)(2,1)S(1)}, bf16[256,640]{1,0:T(8,128)(2,1)}, u32[]{:S(2)}) copy-start(bf16[256,640]{1,0:T(8,128)(2,1)} %cot_hbm.1) | copy-start | bytes 983044
  2.8 0.9 copy-start.2
  3.6 0.7 copy-start.3
  4.3 0.7 copy-start.4

commit v3 on v2

--- a/solution.py
+++ b/solution.py
@@ -6,7 +6,7 @@
 from jax.sharding import PartitionSpec as P
 
 QBLOCK = 128
-VMEM = 40 << 20
+VMEM = 58 << 20
 NY, NZ, NX = 8, 4, 4
 HERE = NY // 2
 PARTS = 2
@@ -349,21 +349,22 @@
     tok_from_z(1)
     cot_step(2)
     tok_from_z(2)
+    weights_other()
+    tg_part(0)
     tok_from_x(0)
+    tg_part(1)
+    tg_part(-1)
+    cot_step(3)
+    tok_from_x(1)
     tok_from_z(3)
-    cot_step(3)
-    weights_other()
-    for i in (0, 1, -1):
-        tg_part(i)
-    tok_from_x(1)
-    for i in (0, 1, -1):
-        tg_sum(i)
+    tg_sum(0)
+    tg_sum(1)
+    tg_sum(-1)
     cot_step(4)
-    for i in (2, -2):
-        tg_part(i)
     tok_from_x(2)
-    for e in (0, 1, 7):
-        tok_from_core(e)
+    tok_from_core(0)
+    tok_from_core(1)
+    tok_from_core(7)
     product(4)
     ring_start(0, 0)
     ring_start(1, 0)
@@ -371,36 +372,40 @@
     ring_start(0, 1)
     product(-3)
     ring_start(1, 1)
+    tg_part(2)
+    tg_part(-2)
+    tg_sum(2)
+    tg_sum(-2)
+    cot_step(5)
+    tg_part(3)
+    tg_part(-3)
     tok_from_x(3)
-    for i in (2, -2):
-        tg_sum(i)
-    cot_step(5)
-    for i in (3, -3):
-        tg_part(i)
+    tg_sum(3)
+    tg_sum(-3)
     cot_step(6)
     tg_part(4)
-    for e in (6, 2):
-        tok_from_core(e)
+    tok_from_core(6)
+    tok_from_core(2)
+    tg_sum(4)
     product(2)
     product(-2)
-    for i in (3, -3, 4):
-        tg_sum(i)
     ring_step(0)
-    for e in (5, 3, 4):
-        tok_from_core(e)
+    tg_from_x(2)
+    tok_from_core(5)
+    tok_from_core(3)
+    tok_from_core(4)
     wg_start()
-    tg_from_x(2)
     ring_step(1)
+    tg_from_x(1)
+    tg_from_x(3)
     product(1)
     product(-1)
-    tg_from_x(1)
-    tg_from_x(3)
     ring_step(2)
-    tg_from_x(0)
     product(0)
     ring_step(3)
+    tg_from_x(0)
+    ring_step(4)
     tg_from_z()
-    ring_step(4)
     wg_own()
     wg_end()
     ring_step(5)

time: 94.9 us -> 92.8 us (0.978)
  the two profiles are of different devices: /device:TPU:1 before, /device:TPU:26 now
where the time goes in v3:
time: 92.8 us; the launch traced here: 92.7 us
  Pallas kernels  87.8 us (95%)
  local copies, waits for them, and re-layouts  4.22 us (5%)
    pallas_call x1, Pallas kernels, on_device(): pl.pallas_call(kernel, name='up_projection', out_shape=(jax.ShapeDtypeStr...  87.8 us
    unnamed x5, local copies, waits for them, and re-layouts  4.22 us

profile of v3, /device:TPU:26, one launch (start us, length us, event | category | flops | bytes accessed | tf_op | source)
XLA Modules:
  0.0 92.7 jit_solution(1747917325306487556)
XLA Ops:
  0.6 87.8 %up_projection.1 = (bf16[256,640]{1,0:T(8,128)(2,1)}, bf16[160,256]{1,0:T(8,128)(2,1)}, f32[320,640]{1,0:T(8,128)}) custom-call(bf16[160,256]{1,0:T(8,128)(2,1)} %bitcast.4, s32[320,640]{1,0:T(8,128)} %code_hbm.1, f32[5,320]{1,0:T(8,128)} %bitcast.6, bf16[256,640]{1,0:T(8,128)(2,1)} %cot_hbm.1, s32[5,320]{1,0:T(8,128)} %bitcast.7), custom_call_target="tpu_custom_call" | custom-call | tf_op jit(solution)/shard_map/up_projection/pallas_call | solution.py:472
  88.4 0.0 copy-start
  88.4 1.8 %copy.11 = bf16[256,640]{1,0:T(8,128)(2,1)} copy(bf16[256,640]{1,0:T(8,128)(2,1)} %get-tuple-element.12) | data formatting | bytes 655360
  90.2 1.5 %copy.12 = bf16[256,160]{0,1:T(8,128)(2,1)} copy(bf16[256,160]{0,1:T(8,128)(2,1)} %bitcast.5) | data formatting | bytes 163840
  91.8 0.0 copy-done
  91.8 0.9 copy.13
Async XLA Ops:
  88.4 3.3 %copy-start = (f32[320,640]{1,0:T(8,128)S(1)}, f32[320,640]{1,0:T(8,128)}, u32[]{:S(2)}) copy-start(f32[320,640]{1,0:T(8,128)} %get-tuple-element.14) | copy-start | bytes 2457604

commit v4 on v3

--- a/solution.py
+++ b/solution.py
@@ -17,9 +17,9 @@
 def kernel(
     tok_hbm, code_hbm, scale_hbm, cot_hbm, exp_hbm,
     out_ref, tgrad_ref, wgrad_ref,
-    tok, code, scale, expo, wts, cot, feats, narrow, part, from_core, summed,
-    from_x, reduced, from_z, final, home, prod, ring, wg_send, wg_recv,
-    in_s, to_s, to_r, cot_s, cot_r, one_s, one_r, tz_s, tz_r, tx_s, tx_r, tk_s, tk_r,
+    tok, code, scale, expo, held, wts, cot, feats, narrow, part, from_core, summed,
+    from_x, reduced, from_z, final, back, home, prod, ring, wg_send, wg_recv,
+    in_s, ta_s, ta_r, to_s, to_r, cot_s, cot_r, one_s, one_r, tz_s, tz_r, tx_s, tx_r, tk_s, tk_r,
     gk_s, gk_r, gx_s, gx_r, gz_s, gz_r, ring_s, ring_r,
 ):
     node, cross = lax.axis_index("node"), lax.axis_index("cross")
@@ -49,10 +49,12 @@
     zs = [at(zh=(zh + o) % NZ) for o in range(1, NZ)]
     xs = [at(x=(x + o) % NX) for o in range(1, NX)]
     place = 2 * zh + x // 2
-    slot_there = (y - place + HERE + NY) % NY
-    owner = at(y=place, zh=slot_there // 2, x=2 * (slot_there % 2) + x % 2)
-    home_of = at(y=(y + NY - HERE + place) % NY, zh=y // 2, x=2 * (y % 2) + x % 2)
-    moves = jnp.logical_or(place != y, place != HERE)
+    goal = (y - place + HERE + NY) % NY
+    turn = at(zh=goal // 2, x=2 * (goal % 2) + x % 2)
+    turns = goal != place
+    fore = at(y=(y + NY + HERE - place) % NY)
+    aft = at(y=(y + NY - HERE + place) % NY)
+    shifts = place != HERE
 
     def remote(src, dst, send, recv, device):
         return pltpu.make_async_remote_copy(
@@ -84,12 +86,18 @@
     for device in friends:
         greet(device)
 
-    @pl.when(moves)
+    @pl.when(turns)
     def _():
-        greet(owner)
-        greet(home_of)
-
-    pl.semaphore_wait(barrier, len(friends) + 2 * moves.astype(jnp.int32))
+        greet(turn)
+
+    @pl.when(shifts)
+    def _():
+        greet(fore)
+        greet(aft)
+
+    pl.semaphore_wait(
+        barrier, len(friends) + turns.astype(jnp.int32) + 2 * shifts.astype(jnp.int32)
+    )
 
     size = own // PARTS
 
@@ -98,20 +106,39 @@
         return feats.at[e, pl.ds(pl.multiple_of(start, 16), own if p is None else size)]
 
     own_g = 2 * (x % 2) + k
-    to_owner = [
-        remote(tok.at[pl.ds(p * size, size)], spot(slot_there, own_g, p), to_s.at[p], to_r.at[p], owner)
+    bits = [pl.ds(p * size, size) for p in range(PARTS)]
+    to_turn = [
+        remote(tok.at[bits[p]], held.at[bits[p]], ta_s.at[p], ta_r.at[p], turn)
         for p in range(PARTS)
     ]
+    to_fore = [
+        remote(held.at[bits[p]], spot(place, own_g, p), to_s.at[p], to_r.at[p], fore)
+        for p in range(PARTS)
+    ]
 
     def tok_start():
-        @pl.when(moves)
-        def _():
-            for copy in to_owner:
+        @pl.when(turns)
+        def _():
+            for copy in to_turn:
                 copy.start()
 
-        @pl.when(jnp.logical_not(moves))
-        def _():
-            spot(place, own_g)[...] = tok[...]
+        @pl.when(jnp.logical_not(turns))
+        def _():
+            held[...] = tok[...]
+
+    def tok_shift():
+        for p in range(PARTS):
+            @pl.when(turns)
+            def _():
+                landed(held.at[bits[p]], ta_r.at[p])
+
+            @pl.when(shifts)
+            def _():
+                to_fore[p].start()
+
+            @pl.when(jnp.logical_not(shifts))
+            def _():
+                spot(place, own_g, p)[...] = held[bits[p]]
 
     def tok_send_x(j, p):
         src = spot(2 * j + x // 2, own_g, p)
@@ -126,7 +153,7 @@
         for p in range(PARTS):
             src = spot(place, own_g, p)
 
-            @pl.when(moves)
+            @pl.when(shifts)
             def _():
                 landed(src, to_r.at[p])
 
@@ -258,7 +285,8 @@
         def _():
             copy.start()
 
-    to_home = remote(final, home, one_s.at[2], one_r.at[2], home_of)
+    to_aft = remote(final, back, one_s.at[2], one_r.at[2], aft)
+    to_home = remote(back, home, one_s.at[0], one_r.at[0], turn)
 
     def tg_from_z():
         total = reduced[zh].astype(F32)
@@ -267,19 +295,32 @@
             total += from_z[o].astype(F32)
         final[...] = total.astype(BF16)
 
-        @pl.when(moves)
+        @pl.when(shifts)
+        def _():
+            to_aft.start()
+
+    def tg_turn():
+        @pl.when(shifts)
+        def _():
+            to_aft.wait_recv()
+
+        @pl.when(jnp.logical_not(shifts))
+        def _():
+            back[...] = final[...]
+
+        @pl.when(turns)
         def _():
             to_home.start()
 
     def tg_end():
-        @pl.when(moves)
+        @pl.when(turns)
         def _():
             to_home.wait_recv()
             tgrad_ref[...] = home[...]
 
-        @pl.when(jnp.logical_not(moves))
-        def _():
-            tgrad_ref[...] = final[...]
+        @pl.when(jnp.logical_not(turns))
+        def _():
+            tgrad_ref[...] = back[...]
 
     def product(i):
         e = (HERE + i) % NY
@@ -343,6 +384,7 @@
     weights_own()
     weights_send()
     loads[4].wait()
+    tok_shift()
     cot_step(0)
     tok_own()
     cot_step(1)
@@ -357,21 +399,21 @@
     cot_step(3)
     tok_from_x(1)
     tok_from_z(3)
+    cot_step(4)
+    tok_from_core(0)
+    tok_from_core(1)
+    product(4)
+    ring_start(0, 0)
+    ring_start(1, 0)
+    product(-3)
+    ring_start(1, 1)
     tg_sum(0)
     tg_sum(1)
     tg_sum(-1)
-    cot_step(4)
     tok_from_x(2)
-    tok_from_core(0)
-    tok_from_core(1)
     tok_from_core(7)
-    product(4)
-    ring_start(0, 0)
-    ring_start(1, 0)
     product(3)
     ring_start(0, 1)
-    product(-3)
-    ring_start(1, 1)
     tg_part(2)
     tg_part(-2)
     tg_sum(2)
@@ -402,14 +444,14 @@
     product(-1)
     ring_step(2)
     product(0)
+    tg_from_x(0)
     ring_step(3)
-    tg_from_x(0)
     ring_step(4)
     tg_from_z()
     wg_own()
+    tg_turn()
     wg_end()
     ring_step(5)
-    tg_end()
     ring_step(6)
     for h in range(2):
         out_ref[hs[h]] = (
@@ -418,11 +460,14 @@
             + ring[1, 7 + h].astype(F32)
         ).astype(BF16)
 
+    tg_end()
+
     for copy in started:
         copy.wait_send()
     some = [tg_x_copy(e, xl) for e in range(NY) for xl in range(2)]
     some += [tg_z_copy(j) for j in range(NZ)]
-    some += [(moves, copy) for copy in to_owner + [to_home]]
+    some += [(turns, copy) for copy in to_turn + [to_home]]
+    some += [(shifts, copy) for copy in to_fore + [to_aft]]
     for leaves, copy in some:
 
         @pl.when(leaves)
@@ -441,6 +486,7 @@
         pltpu.VMEM((rows, width), jnp.int32),
         pltpu.VMEM((width // QBLOCK, rows), F32),
         pltpu.VMEM((width // QBLOCK, rows), jnp.int32),
+        pltpu.VMEM((own, count), BF16),
         pltpu.VMEM((depth, width), BF16),
         pltpu.VMEM((NY, count, width), BF16),
         pltpu.VMEM((NY, depth, count), BF16),
@@ -453,11 +499,13 @@
         pltpu.VMEM((NZ - 1, own, count), BF16),
         pltpu.VMEM((own, count), BF16),
         pltpu.VMEM((own, count), BF16),
+        pltpu.VMEM((own, count), BF16),
         pltpu.VMEM((NY, count, width), F32),
         pltpu.VMEM((2, 9, count // 2, width), BF16),
         pltpu.VMEM((rows, width), BF16),
         pltpu.VMEM((rows, width), BF16),
         dma((5,)),
+        dma((PARTS,)), dma((PARTS,)),
         dma((PARTS,)), dma((PARTS,)),
         dma((2, 2, 4)), dma((2, 2, 4)),
         dma((4,)), dma((4,)),

time: 92.8 us -> 90.6 us (0.976)
  the two profiles are of different devices: /device:TPU:26 before, /device:TPU:42 now
where the time goes in v4:
time: 90.6 us; the launch traced here: 90.4 us
  Pallas kernels  85.5 us (94%)
  local copies, waits for them, and re-layouts  4.22 us (5%)
    pallas_call x1, Pallas kernels, on_device(): pl.pallas_call(kernel, name='up_projection', out_shape=(jax.ShapeDtypeStr...  85.5 us
    unnamed x5, local copies, waits for them, and re-layouts  4.22 us

profile of v4, /device:TPU:42, one launch (start us, length us, event | category | flops | bytes accessed | tf_op | source)
XLA Modules:
  0.0 90.4 jit_solution(14876531589199872445)
XLA Ops:
  0.6 85.5 %up_projection.1 = (bf16[256,640]{1,0:T(8,128)(2,1)}, bf16[160,256]{1,0:T(8,128)(2,1)}, f32[320,640]{1,0:T(8,128)}) custom-call(bf16[160,256]{1,0:T(8,128)(2,1)} %bitcast.4, s32[320,640]{1,0:T(8,128)} %code_hbm.1, f32[5,320]{1,0:T(8,128)} %bitcast.6, bf16[256,640]{1,0:T(8,128)(2,1)} %cot_hbm.1, s32[5,320]{1,0:T(8,128)} %bitcast.7), custom_call_target="tpu_custom_call" | custom-call | tf_op jit(solution)/shard_map/up_projection/pallas_call | solution.py:520
  86.2 0.0 copy-start
  86.2 1.8 %copy.11 = bf16[256,640]{1,0:T(8,128)(2,1)} copy(bf16[256,640]{1,0:T(8,128)(2,1)} %get-tuple-element.12) | data formatting | bytes 655360
  88.0 1.5 %copy.12 = bf16[256,160]{0,1:T(8,128)(2,1)} copy(bf16[256,160]{0,1:T(8,128)(2,1)} %bitcast.5) | data formatting | bytes 163840
  89.5 0.0 copy-done
  89.5 0.9 copy.13
Async XLA Ops:
  86.2 3.3 %copy-start = (f32[320,640]{1,0:T(8,128)S(1)}, f32[320,640]{1,0:T(8,128)}, u32[]{:S(2)}) copy-start(f32[320,640]{1,0:T(8,128)} %get-tuple-element.14) | copy-start | bytes 2457604

commit v5 on v4

--- a/solution.py
+++ b/solution.py
@@ -376,6 +376,19 @@
             wgrad_ref[:, cols] = (
                 wgrad_ref[:, cols] + wg_recv[:, cols].astype(F32)
             ) * factor[:, b : b + 1]
+
+    def all_left():
+        for copy in started:
+            copy.wait_send()
+        some = [tg_x_copy(e, xl) for e in range(NY) for xl in range(2)]
+        some += [tg_z_copy(j) for j in range(NZ)]
+        some += [(turns, copy) for copy in to_turn]
+        some += [(shifts, copy) for copy in to_fore + [to_aft]]
+        for leaves, copy in some:
+
+            @pl.when(leaves)
+            def _():
+                copy.wait_send()
 
     loads[0].wait()
     tok_start()
@@ -450,6 +463,7 @@
     tg_from_z()
     wg_own()
     tg_turn()
+    all_left()
     wg_end()
     ring_step(5)
     ring_step(6)
@@ -462,17 +476,9 @@
 
     tg_end()
 
-    for copy in started:
-        copy.wait_send()
-    some = [tg_x_copy(e, xl) for e in range(NY) for xl in range(2)]
-    some += [tg_z_copy(j) for j in range(NZ)]
-    some += [(turns, copy) for copy in to_turn + [to_home]]
-    some += [(shifts, copy) for copy in to_fore + [to_aft]]
-    for leaves, copy in some:
-
-        @pl.when(leaves)
-        def _():
-            copy.wait_send()
+    @pl.when(turns)
+    def _():
+        to_home.wait_send()
 
 
 def on_device(tokens, weight_codes, weight_scales, cotangent, grad_exponents):

time: 90.6 us -> 90.5 us (level)
  the two profiles are of different devices: /device:TPU:42 before, /device:TPU:24 now
where the time goes in v5:
time: 90.5 us; the launch traced here: 90.4 us
  Pallas kernels  85.5 us (94%)
  local copies, waits for them, and re-layouts  4.22 us (5%)
    pallas_call x1, Pallas kernels, on_device(): pl.pallas_call(kernel, name='up_projection', out_shape=(jax.ShapeDtypeStr...  85.5 us
    unnamed x5, local copies, waits for them, and re-layouts  4.22 us

profile of v5, /device:TPU:24, one launch (start us, length us, event | category | flops | bytes accessed | tf_op | source)
XLA Modules:
  0.0 90.4 jit_solution(14178048569002166773)
XLA Ops:
  0.6 85.5 %up_projection.1 = (bf16[256,640]{1,0:T(8,128)(2,1)}, bf16[160,256]{1,0:T(8,128)(2,1)}, f32[320,640]{1,0:T(8,128)}) custom-call(bf16[160,256]{1,0:T(8,128)(2,1)} %bitcast.4, s32[320,640]{1,0:T(8,128)} %code_hbm.1, f32[5,320]{1,0:T(8,128)} %bitcast.6, bf16[256,640]{1,0:T(8,128)(2,1)} %cot_hbm.1, s32[5,320]{1,0:T(8,128)} %bitcast.7), custom_call_target="tpu_custom_call" | custom-call | tf_op jit(solution)/shard_map/up_projection/pallas_call | solution.py:526
  86.1 0.0 copy-start
  86.1 1.8 %copy.11 = bf16[256,640]{1,0:T(8,128)(2,1)} copy(bf16[256,640]{1,0:T(8,128)(2,1)} %get-tuple-element.12) | data formatting | bytes 655360
  87.9 1.5 %copy.12 = bf16[256,160]{0,1:T(8,128)(2,1)} copy(bf16[256,160]{0,1:T(8,128)(2,1)} %bitcast.5) | data formatting | bytes 163840
  89.5 0.0 copy-done
  89.5 0.9 copy.13
Async XLA Ops:
  86.1 3.3 %copy-start = (f32[320,640]{1,0:T(8,128)S(1)}, f32[320,640]{1,0:T(8,128)}, u32[]{:S(2)}) copy-start(f32[320,640]{1,0:T(8,128)} %get-tuple-element.14) | copy-start | bytes 2457604
